TPU v7x, 32 devices: a whole 2x2x4 slice. The times are simulated.
32 devices in a mesh: dp: 4 (over z), ctx: 8 (over y, x, core).
Axes of the slice: x: 2, y: 2, z: 4, core: 2. Of those that a mesh axis runs over, the one named last changes fastest.
Arguments:
- frames: bfloat16 [4, 1024, 512], P('dp', 'ctx'), may hold values from -6 to 6
- conv_weight: bfloat16 [3, 512, 512], replicated, may hold values from -0.15625 to 0.15625
- proj_weight: bfloat16 [512, 768], replicated, may hold values from -0.25 to 0.25
- query_weight: bfloat16 [768, 384], replicated, may hold values from -1.5 to 1.5
- key_weight: bfloat16 [768, 384], replicated, may hold values from -1.5 to 1.5
- value_weight: bfloat16 [768, 384], replicated, may hold values from -0.21875 to 0.21875
- cotangent: bfloat16 [4, 512, 384], P('dp', 'ctx'), may hold values from -6 to 6
Outputs:
- weight_grad: float32 [1536, 512], P('ctx', 'dp')
- frame_grad: bfloat16 [4, 1024, 512], P('dp', 'ctx')
All inputs are finite; a program needn't handle non-finite values.
Results may differ from a plain program's by a relative error of at most 0.04.
Values may be sent and summed in bfloat16 or wider, within the bound.
A program may use at most 64 MiB of HBM per device.

v0:
```python
import math
import jax
import jax.numpy as jnp
from jax import lax
from jax.sharding import PartitionSpec as P

HEADS = 6
HEAD_DIM = 64
SQRT_HALF = 0.7071067811865476
INV_ROOT_TAU = 0.3989422804014327
EPSILON = 1e-05


def from_behind(value, axis, steps):
    count = lax.axis_size(axis)
    initial, last = (max(0, -steps), min(count, count - steps))
    return lax.ppermute(value, axis, [(source, source + steps) for source in range(initial, last)])


def gelu_slope(pre):
    return 0.5 * (1.0 + lax.erf(pre * SQRT_HALF)) + pre * INV_ROOT_TAU * jnp.exp(-0.5 * pre * pre)


def blocked(step_fn, carry, piece):
    rows = piece[0].shape[0]
    block_rows = math.gcd(rows, 512)
    block_count = rows // block_rows
    stacked = tuple(
        (member.reshape((block_count, block_rows) + member.shape[1:]) for member in piece)
    )

    def inner(state, item):
        block_index, members = item
        return (step_fn(state, members, block_index * block_rows), None)

    final, unused = lax.scan(inner, carry, (jnp.arange(block_count, dtype=jnp.int32), stacked))
    return final


def local(frames, conv_weight, proj_weight, query_weight, key_weight, value_weight, cotangent):
    inputs = frames[0]
    count = inputs.shape[0] // 2
    width = inputs.shape[1]
    following = from_behind(inputs[:1], "ctx", -1)
    paired = inputs.reshape(count, 2, width)
    tap_first = paired[:, 0]
    tap_second = paired[:, 1]
    tap_third = jnp.concatenate([tap_first[1:], following], 0)
    conv_out = jnp.dot(tap_first, conv_weight[0], preferred_element_type=jnp.float32)
    conv_out = conv_out + jnp.dot(tap_second, conv_weight[1], preferred_element_type=jnp.float32)
    conv_out = conv_out + jnp.dot(tap_third, conv_weight[2], preferred_element_type=jnp.float32)
    activated = jax.nn.gelu(conv_out, approximate=False)
    centre = jnp.mean(activated, -1, keepdims=True)
    spread = jnp.mean((activated - centre) ** 2, -1, keepdims=True)
    inv_std = lax.rsqrt(spread + EPSILON)
    normed = (activated - centre) * inv_std
    hidden = jnp.dot(
        normed.astype(jnp.bfloat16), proj_weight, preferred_element_type=jnp.float32
    ).astype(jnp.bfloat16)
    queries = jnp.dot(hidden, query_weight, preferred_element_type=jnp.float32).astype(jnp.bfloat16)
    keys = jnp.dot(hidden, key_weight, preferred_element_type=jnp.float32).astype(jnp.bfloat16)
    values = jnp.dot(hidden, value_weight, preferred_element_type=jnp.float32).astype(jnp.bfloat16)
    upstream = cotangent[0]
    scale = HEAD_DIM ** (-0.5)
    query_heads = queries.reshape(count, HEADS, HEAD_DIM)
    key_heads = keys.reshape(count, HEADS, HEAD_DIM)
    value_heads = values.reshape(count, HEADS, HEAD_DIM)
    grad_heads = upstream.reshape(count, HEADS, HEAD_DIM)

    def forward_block(carry, piece, start):
        running_top, running_total, accum = carry
        rows = piece[0].shape[0]
        keys_part = piece[0].reshape(rows, HEADS, HEAD_DIM)
        values_part = piece[1].reshape(rows, HEADS, HEAD_DIM)
        scores = (
            jnp.einsum("qhe,khe->hqk", query_heads, keys_part, preferred_element_type=jnp.float32)
            * scale
        )
        new_top = jnp.maximum(running_top, jnp.max(scores, -1))
        factor = jnp.exp(running_top - new_top)
        weights = jnp.exp(scores - new_top[:, :, None])
        new_total = running_total * factor + jnp.sum(weights, -1)
        new_accum = accum * jnp.transpose(factor)[:, :, None] + jnp.einsum(
            "hqk,khe->qhe",
            weights,
            values_part.astype(jnp.float32),
            precision=lax.Precision.HIGHEST,
        )
        return (new_top, new_total, new_accum)

    start_state = (
        jnp.full((HEADS, count), -jnp.inf, jnp.float32),
        jnp.zeros((HEADS, count), jnp.float32),
        jnp.zeros((count, HEADS, HEAD_DIM), jnp.float32),
    )
    final_top, final_total, final_accum = blocked(
        forward_block,
        start_state,
        (
            lax.all_gather(keys, "ctx", axis=0, tiled=True),
            lax.all_gather(values, "ctx", axis=0, tiled=True),
        ),
    )
    lse_heads = final_top + jnp.log(final_total)
    outputs = final_accum / jnp.transpose(final_total)[:, :, None]
    delta_rows = jnp.sum(grad_heads.astype(jnp.float32) * outputs, -1)
    delta_heads = jnp.transpose(delta_rows)

    def query_block(carry, piece, start):
        rows = piece[0].shape[0]
        keys_part = piece[0].reshape(rows, HEADS, HEAD_DIM)
        values_part = piece[1].reshape(rows, HEADS, HEAD_DIM)
        scores = (
            jnp.einsum("qhe,khe->hqk", query_heads, keys_part, preferred_element_type=jnp.float32)
            * scale
        )
        probs = jnp.exp(scores - lse_heads[:, :, None])
        prob_grad = jnp.einsum(
            "qhe,khe->hqk", grad_heads, values_part, preferred_element_type=jnp.float32
        )
        score_grad = probs * (prob_grad - delta_heads[:, :, None])
        return carry + jnp.einsum(
            "hqk,khe->qhe",
            score_grad.astype(jnp.bfloat16),
            keys_part,
            preferred_element_type=jnp.float32,
        )

    query_start = jnp.zeros((count, HEADS, HEAD_DIM), jnp.float32)
    query_accum = blocked(
        query_block,
        query_start,
        (
            lax.all_gather(keys, "ctx", axis=0, tiled=True),
            lax.all_gather(values, "ctx", axis=0, tiled=True),
        ),
    )
    query_grad = (query_accum * scale).astype(jnp.bfloat16).reshape(count, HEADS * HEAD_DIM)
    all_lse, all_delta = (
        lax.all_gather(jnp.transpose(lse_heads), "ctx", axis=0, tiled=True),
        lax.all_gather(delta_rows, "ctx", axis=0, tiled=True),
    )

    def key_block(carry, piece, start):
        key_accum, value_accum = carry
        rows = piece[0].shape[0]
        query_part = piece[0].reshape(rows, HEADS, HEAD_DIM)
        grad_part = piece[1].reshape(rows, HEADS, HEAD_DIM)
        lse_part = jnp.transpose(lax.dynamic_slice_in_dim(all_lse, start, rows, 0))
        delta_part = jnp.transpose(lax.dynamic_slice_in_dim(all_delta, start, rows, 0))
        scores = (
            jnp.einsum("qhe,khe->hqk", query_part, key_heads, preferred_element_type=jnp.float32)
            * scale
        )
        probs = jnp.exp(scores - lse_part[:, :, None])
        value_accum = value_accum + jnp.einsum(
            "hqk,qhe->khe",
            probs.astype(jnp.bfloat16),
            grad_part,
            preferred_element_type=jnp.float32,
        )
        prob_grad = jnp.einsum(
            "qhe,khe->hqk", grad_part, value_heads, preferred_element_type=jnp.float32
        )
        score_grad = probs * (prob_grad - delta_part[:, :, None])
        key_accum = key_accum + jnp.einsum(
            "hqk,qhe->khe",
            score_grad.astype(jnp.bfloat16),
            query_part,
            preferred_element_type=jnp.float32,
        )
        return (key_accum, value_accum)

    key_start = (
        jnp.zeros((count, HEADS, HEAD_DIM), jnp.float32),
        jnp.zeros((count, HEADS, HEAD_DIM), jnp.float32),
    )
    key_accum, value_accum = blocked(
        key_block,
        key_start,
        (
            lax.all_gather(queries, "ctx", axis=0, tiled=True),
            lax.all_gather(upstream, "ctx", axis=0, tiled=True),
        ),
    )
    key_grad = (key_accum * scale).astype(jnp.bfloat16).reshape(count, HEADS * HEAD_DIM)
    value_grad = value_accum.astype(jnp.bfloat16).reshape(count, HEADS * HEAD_DIM)
    hidden_grad = jnp.einsum(
        "tk,dk->td", query_grad, query_weight, preferred_element_type=jnp.float32
    )
    hidden_grad = hidden_grad + jnp.einsum(
        "tk,dk->td", key_grad, key_weight, preferred_element_type=jnp.float32
    )
    hidden_grad = hidden_grad + jnp.einsum(
        "tk,dk->td", value_grad, value_weight, preferred_element_type=jnp.float32
    )
    hidden_grad = hidden_grad.astype(jnp.bfloat16)
    normed_grad = jnp.einsum(
        "td,cd->tc", hidden_grad, proj_weight, preferred_element_type=jnp.float32
    )
    act_grad = inv_std * (
        normed_grad
        - jnp.mean(normed_grad, -1, keepdims=True)
        - normed * jnp.mean(normed_grad * normed, -1, keepdims=True)
    )
    conv_grad = (act_grad * gelu_slope(conv_out)).astype(jnp.bfloat16)
    kernel_terms = jnp.concatenate(
        [
            jnp.einsum("tc,to->co", tap_first, conv_grad, preferred_element_type=jnp.float32),
            jnp.einsum("tc,to->co", tap_second, conv_grad, preferred_element_type=jnp.float32),
            jnp.einsum("tc,to->co", tap_third, conv_grad, preferred_element_type=jnp.float32),
        ],
        0,
    )
    earlier = from_behind(conv_grad[count - 1 :], "ctx", 1)
    first = jnp.einsum("to,co->tc", conv_grad, conv_weight[0], preferred_element_type=jnp.float32)
    second = jnp.einsum("to,co->tc", conv_grad, conv_weight[1], preferred_element_type=jnp.float32)
    third = jnp.einsum("to,co->tc", conv_grad, conv_weight[2], preferred_element_type=jnp.float32)
    incoming = jnp.einsum("to,co->tc", earlier, conv_weight[2], preferred_element_type=jnp.float32)
    moved = jnp.concatenate([incoming, third[:-1]], 0)
    even_rows = first + moved
    frame_rows = jnp.stack([even_rows, second], 1).reshape(2 * count, width).astype(jnp.bfloat16)
    frame_sum = lax.psum_scatter(
        kernel_terms.astype(jnp.bfloat16), "ctx", scatter_dimension=0, tiled=True
    )
    weight_grad = lax.psum_scatter(frame_sum, "dp", scatter_dimension=1, tiled=True).astype(
        jnp.float32
    )
    return (weight_grad, frame_rows[None])


def solution(mesh):
    in_specs = (P("dp", "ctx", None), P(), P(), P(), P(), P(), P("dp", "ctx", None))
    out_specs = (P("ctx", "dp"), P("dp", "ctx", None))
    return jax.shard_map(local, mesh=mesh, in_specs=in_specs, out_specs=out_specs, check_vma=False)
```

profile of v0, /device:TPU:0, one launch (start us, length us, event | category | flops | bytes accessed | tf_op | source)
XLA Modules:
  0.0 179.6 jit_solution(5564387920158402411)
XLA Ops:
  7.2 0.8 slice_bitcast_fusion
  8.0 1.3 collective-permute-start
  9.3 1.0 reshape_squeeze.6
  10.5 1.4 fusion.36
  11.9 1.2 convolution_add_fusion.3
  13.1 12.5 %all-gather = bf16[1,512,384]{2,1,0:T(8,128)(2,1)S(1)} all-gather(bf16[1,64,384]{2,1,0:T(8,128)(2,1)S(1)} %copy-done.17), channel_id=2, replica_groups=mesh['dp'=4,'ctx'=8] {'ctx'}, dimensions={1}, use_global_device_ids=true | all-gather | bytes 442368 | tf_op jit(solution)/shard_map/all_gather | solution.py:183
  25.8 0.7 copy.41
  26.7 0.4 copy-done.15
  27.2 1.2 fusion.90
  28.6 0.4 copy-done.19
  29.0 0.5 copy-done.21
  30.1 0.6 copy-done.11
  30.7 9.7 %all_gather.20 = bf16[512,384]{1,0:T(8,128)(2,1)} all-gather(bf16[64,384]{1,0:T(8,128)(2,1)S(1)} %convolution_convert_fusion.8), channel_id=1, replica_groups=mesh['dp'=4,'ctx'=8] {'ctx'}, dimensions={0}, use_global_device_ids=true | all-gather | bytes 442368 | tf_op jit(solution)/shard_map/all_gather | solution.py:134
  40.3 1.9 %copy.38 = bf16[512,384]{0,1:T(8,128)(2,1)} copy(bf16[512,384]{1,0:T(8,128)(2,1)} %all_gather.20) | data formatting | bytes 786432 | tf_op jit(solution)/shard_map/all_gather | solution.py:134
  42.5 0.8 reshape.115
  43.3 1.4 fusion.93
  44.9 0.6 fusion.85
  45.5 10.4 %all_gather.22 = bf16[512,384]{1,0:T(8,128)(2,1)} all-gather(bf16[64,384]{1,0:T(8,128)(2,1)S(1)} %copy-done.13), channel_id=1, replica_groups=mesh['dp'=4,'ctx'=8] {'ctx'}, dimensions={0}, use_global_device_ids=true | all-gather | bytes 442368 | tf_op jit(solution)/shard_map/all_gather | solution.py:182
  56.0 1.6 reshape.119
  57.6 1.3 convolution_convert_fusion.6
  58.9 0.6 copy-done.14
  59.5 9.7 %all_gather.21 = bf16[512,384]{1,0:T(8,128)(2,1)} all-gather(bf16[64,384]{1,0:T(8,128)(2,1)S(1)} %convolution_convert_fusion.6), channel_id=1, replica_groups=mesh['dp'=4,'ctx'=8] {'ctx'}, dimensions={0}, use_global_device_ids=true | all-gather | bytes 442368 | tf_op jit(solution)/shard_map/all_gather | solution.py:135
  69.2 1.6 reshape.120
  70.8 1.9 %copy.40 = bf16[512,384]{0,1:T(8,128)(2,1)} copy(bf16[512,384]{1,0:T(8,128)(2,1)} %all_gather.21) | data formatting | bytes 786432 | tf_op jit(solution)/shard_map/all_gather | solution.py:135
  72.7 1.7 fusion.20
  74.4 2.3 %fusion.19 = bf16[6,64,64]{2,1,0:T(8,128)(2,1)} fusion(bf16[512,6,64]{0,2,1:T(8,128)(2,1)} %bitcast.157, bf16[512,6,64]{0,2,1:T(8,128)(2,1)} %bitcast.161, bf16[64,6,64]{0,2,1:T(8,128)(2,1)} %bitcast.166, f32[6,64,512]{2,1,0:T(8,128)S(1)} %get-tuple-element.67, f32[6,64]{1,0:T(8,128)S(1)} %bitcast.170, f32[6,64]{1,0:T(8,128)S(1)} %log_add_fusion), kind=kOutput, calls=%fused_computation.30 | convolution fusion | flops 51167232 | bytes 1674240 | tf_op jit(solution)/shard_map/while/body/eval_jaxpr/hqk,khe->qhe/dot_general | solution.py:122
  76.7 2.1 %fusion.96 = f32[64,768]{1,0:T(8,128)} fusion(bf16[64,384]{0,1:T(8,128)(2,1)} %bitcast.164, bf16[768,384]{1,0:T(8,128)(2,1)} %param.10), kind=kOutput, calls=%fused_computation.137 | convolution fusion | flops 37748736 | bytes 835584 | tf_op jit(solution)/shard_map/tk,dk->td/dot_general | solution.py:188
  78.8 1.9 %copy.43 = bf16[512,384]{0,1:T(8,128)(2,1)} copy(bf16[512,384]{1,0:T(8,128)(2,1)} %all_gather.22) | data formatting | bytes 786432 | tf_op jit(solution)/shard_map/all_gather | solution.py:182
  80.7 8.9 %all-gather.1 = f32[8,64,6]{1,2,0:T(8,128)S(1)} all-gather(f32[1,64,6]{1,2,0:T(8,128)S(1)} %get-tuple-element.62), channel_id=1, replica_groups=mesh['dp'=4,'ctx'=8] {'ctx'}, dimensions={0}, use_global_device_ids=true | all-gather | bytes 13824 | tf_op jit(solution)/shard_map/all_gather | solution.py:140
  89.7 0.7 reshape.128
  90.4 8.2 %all-gather.2 = f32[8,64,6]{1,2,0:T(8,128)S(1)} all-gather(f32[1,64,6]{1,2,0:T(8,128)S(1)} %bitcast.171), channel_id=1, replica_groups=mesh['dp'=4,'ctx'=8] {'ctx'}, dimensions={0}, use_global_device_ids=true | all-gather | bytes 13824 | tf_op jit(solution)/shard_map/all_gather | solution.py:141
  98.6 1.3 fusion.1
  100.2 0.7 copy.49
  100.9 1.7 reshape.123
  102.6 2.1 %fusion.18 = bf16[6,64,64]{2,1,0:T(8,128)(2,1)} fusion(bf16[512,6,64]{0,2,1:T(8,128)(2,1)} %bitcast.155, f32[6,512,64]{1,2,0:T(8,128)S(1)} %fusion.1, bf16[512,6,64]{0,2,1:T(8,128)(2,1)S(1)} %bitcast.153, f32[6,512]{1,0:T(8,128)S(1)} %bitcast.167, bf16[64,6,64]{2,1,0:T(8,128)(2,1)} %reshape.120), kind=kOutput, calls=%fused_computation.29 | convolution fusion | flops 50970624 | bytes 1683456 | tf_op jit(solution)/shard_map/while/body/eval_jaxpr/hqk,qhe->khe/dot_general | solution.py:166
  104.6 1.5 convolution_add_fusion.1
  106.2 1.8 fusion.89
  108.1 0.3 fusion.9
  108.5 0.3 fusion.8
  108.8 0.3 convolution_convert_fusion
  109.2 1.3 pad_maximum_fusion
  110.5 2.2 %collective-permute-start.1 = (bf16[1,512]{1,0:T(2,128)(2,1)S(1)}, bf16[1,512]{1,0:T(2,128)(2,1)S(1)}, u32[]{:S(2)}, u32[]{:S(2)}) collective-permute-start(bf16[1,512]{1,0:T(2,128)(2,1)S(1)} %slice.53), channel_id=1, source_target_pairs={{0,1},{1,2},{2,3},{3,4},{4,5},{5,6},{6,7},{8,9},{9,10},{10,11},{11... | collective-permute-start | bytes 3080 | tf_op jit(solution)/shard_map/ppermute | solution.py:17
  113.3 36.0 %reduce-scatter.5.cloned.1.call-done = bf16[192,512]{1,0:T(8,128)(2,1)} async-done(((bf16[1536,512]{1,0:T(8,128)(2,1)}), bf16[192,512]{1,0:T(8,128)(2,1)}) %reduce-scatter.5.cloned.1.call-update) | async-done | bytes 196624 | tf_op jit(solution)/shard_map/reduce_scatter | solution.py:223
  149.4 1.8 copy.52
  151.9 0.7 convert_element_type.89
  152.6 18.6 %reduce-scatter.7.cloned.1.call-done = bf16[128,192]{1,0:T(8,128)(2,1)} async-done(((bf16[512,192]{1,0:T(8,128)(2,1)}), bf16[128,192]{1,0:T(8,128)(2,1)}) %reduce-scatter.7.cloned.1.call-update) | async-done | bytes 49168
  171.2 0.9 copy.53
  172.1 0.7 convert_element_type.88
  (76 shorter events, 3.6 us)
Async XLA Ops:
  7.2 22.3 %copy-start = (bf16[512,768]{1,0:T(8,128)(2,1)S(1)}, bf16[512,768]{1,0:T(8,128)(2,1)}, u32[]{:S(2)}) copy-start(bf16[512,768]{1,0:T(8,128)(2,1)} %param.9) | copy-start | bytes 2359300
  7.2 5.9 %copy-start.17 = (bf16[1,64,384]{2,1,0:T(8,128)(2,1)S(1)}, bf16[1,64,384]{2,1,0:T(8,128)(2,1)}, u32[]{:S(2)}) copy-start(bf16[1,64,384]{2,1,0:T(8,128)(2,1)} %param.13) | copy-start | bytes 147460
  7.2 142.2 %reduce-scatter.5.cloned.1.call-start = ((), (), s32[]{:S(2)}) async-start(), calls=%async_computation.2 | async-start | bytes 1769472 | tf_op jit(solution)/shard_map/reduce_scatter | solution.py:223
  8.0 18.7 %collective-permute-start = (bf16[1,512]{1,0:T(2,128)(2,1)S(1)}, bf16[1,512]{1,0:T(2,128)(2,1)S(1)}, u32[]{:S(2)}, u32[]{:S(2)}) collective-permute-start(bf16[1,512]{1,0:T(2,128)(2,1)S(1)} %slice_bitcast_fusion), channel_id=1, source_target_pairs={{1,0},{2,1},{3,2},{4,3},{5,4},{6,5},{7,6},{9,8},{10,9},{11,10},{12... | collective-permute-start | bytes 3080 | tf_op jit(solution)/shard_map/ppermute | solution.py:17
  10.4 1.4 copy-start.7
  10.5 2.7 %copy-start.9 = (bf16[64,1,512]{2,1,0:T(2,128)(2,1)}, bf16[64,1,512]{2,1,0:T(2,128)(2,1)S(1)}, u32[]{:S(2)}) copy-start(bf16[64,1,512]{2,1,0:T(2,128)(2,1)S(1)} %get-tuple-element.60) | copy-start | bytes 196612
  10.5 16.7 %copy-start.1 = (bf16[3,512,512]{2,1,0:T(8,128)(2,1)S(1)}, bf16[3,512,512]{2,1,0:T(8,128)(2,1)}, u32[]{:S(2)}) copy-start(bf16[3,512,512]{2,1,0:T(8,128)(2,1)} %param.8) | copy-start | bytes 4718596
  26.5 0.6 copy-start.15
  26.7 1.6 copy-start.23
  27.2 2.6 %copy-start.3 = (bf16[768,384]{1,0:T(8,128)(2,1)S(1)}, bf16[768,384]{1,0:T(8,128)(2,1)}, u32[]{:S(2)}) copy-start(bf16[768,384]{1,0:T(8,128)(2,1)} %param.11) | copy-start | bytes 1769476
  28.4 1.7 copy-start.4
  28.4 13.9 %copy-start.2 = (bf16[768,384]{1,0:T(8,128)(2,1)S(1)}, bf16[768,384]{1,0:T(8,128)(2,1)}, u32[]{:S(2)}) copy-start(bf16[768,384]{1,0:T(8,128)(2,1)} %param.10) | copy-start | bytes 1769476
  28.4 0.6 copy-start.19
  29.0 0.5 copy-start.21
  29.8 13.5 %copy-start.6 = (bf16[64,768]{1,0:T(8,128)(2,1)}, bf16[64,768]{1,0:T(8,128)(2,1)S(1)}, u32[]{:S(2)}) copy-start(bf16[64,768]{1,0:T(8,128)(2,1)S(1)} %convolution_convert_fusion.4) | copy-start | bytes 294916
  30.0 0.6 copy-start.11
  42.5 0.8 copy-start.12
  43.3 2.3 %copy-start.13 = (bf16[64,384]{1,0:T(8,128)(2,1)S(1)}, bf16[64,384]{1,0:T(8,128)(2,1)}, u32[]{:S(2)}) copy-start(bf16[64,384]{1,0:T(8,128)(2,1)} %copy-done.12) | copy-start | bytes 147460
  58.9 0.6 copy-start.14
  104.6 3.3 %copy-start.5 = (f32[64,512]{1,0:T(8,128)S(1)}, f32[64,512]{1,0:T(8,128)}, u32[]{:S(2)}) copy-start(f32[64,512]{1,0:T(8,128)} %copy-done.4) | copy-start | bytes 393220
  104.6 3.3 %copy-start.18 = (f32[64,512]{1,0:T(8,128)S(1)}, f32[64,512]{1,0:T(8,128)}, u32[]{:S(2)}) copy-start(f32[64,512]{1,0:T(8,128)} %get-tuple-element.65) | copy-start | bytes 393220
  104.6 3.4 %copy-start.20 = (f32[64]{0:T(128)S(1)}, f32[64]{0:T(128)}, u32[]{:S(2)}) copy-start(f32[64]{0:T(128)} %copy-done.19) | copy-start | bytes 772
  104.6 3.4 %copy-start.22 = (f32[64]{0:T(128)S(1)}, f32[64]{0:T(128)}, u32[]{:S(2)}) copy-start(f32[64]{0:T(128)} %copy-done.21) | copy-start | bytes 772
  104.6 3.5 %copy-start.10 = (bf16[64,1,512]{2,1,0:T(2,128)(2,1)S(1)}, bf16[64,1,512]{2,1,0:T(2,128)(2,1)}, u32[]{:S(2)}) copy-start(bf16[64,1,512]{2,1,0:T(2,128)(2,1)} %copy-done.9) | copy-start | bytes 196612
  106.1 2.3 %copy-start.8 = (bf16[64,1,512]{2,1,0:T(2,128)(2,1)S(1)}, bf16[64,1,512]{2,1,0:T(2,128)(2,1)}, u32[]{:S(2)}) copy-start(bf16[64,1,512]{2,1,0:T(2,128)(2,1)} %copy-done.7) | copy-start | bytes 196612
  106.1 2.7 %copy-start.16 = (bf16[63,1,512]{2,0,1:T(8,128)(2,1)S(1)}, bf16[63,1,512]{2,0,1:T(8,128)(2,1)}, u32[]{:S(2)}) copy-start(bf16[63,1,512]{2,0,1:T(8,128)(2,1)} %copy-done.15) | copy-start | bytes 193540
  106.2 2.7 %copy-start.24 = (bf16[1,512]{1,0:T(2,128)(2,1)S(1)}, bf16[1,512]{1,0:T(2,128)(2,1)}, u32[]{:S(2)}) copy-start(bf16[1,512]{1,0:T(2,128)(2,1)} %copy-done.23) | copy-start | bytes 3076
  110.5 60.7 %reduce-scatter.7.cloned.1.call-start = ((), (), s32[]{:S(2)}) async-start(), calls=%async_computation.3 | async-start | bytes 327680
  110.5 40.6 %collective-permute-start.1 = (bf16[1,512]{1,0:T(2,128)(2,1)S(1)}, bf16[1,512]{1,0:T(2,128)(2,1)S(1)}, u32[]{:S(2)}, u32[]{:S(2)}) collective-permute-start(bf16[1,512]{1,0:T(2,128)(2,1)S(1)} %slice.53), channel_id=1, source_target_pairs={{0,1},{1,2},{2,3},{3,4},{4,5},{5,6},{6,7},{8,9},{9,10},{10,11},{11... | collective-permute-start | bytes 3080 | tf_op jit(solution)/shard_map/ppermute | solution.py:17
Sparse Core Ops, SparseCore 0:
  110.6 38.7 reduce-scatter.4
  151.6 19.5 reduce-scatter.6
where the time goes:
time: 180 us
  blocking collectives  59.4 us (33%)
  waiting for transfers between devices  54.7 us (30%)
  matrix products  22.3 us (12%)
  local copies, waits for them, and re-layouts  21.9 us (12%)
  between operations  14.5 us (8%)
  starting transfers between devices  3.59 us (2%)
  other arithmetic  3.13 us (2%)
    reduce_scatter x1, waiting for transfers between devices, local(): lax.psum_scatter(kernel_terms.astype(jnp.bfloat16), 'ctx', scatter_dimens...  36 us
    unnamed x3, waiting for transfers between devices  18.6 us
    all_gather x1, blocking collectives, local(): lax.all_gather(upstream, 'ctx', axis=0, tiled=True)  12.5 us
    all_gather x1, blocking collectives, local(): lax.all_gather(queries, 'ctx', axis=0, tiled=True)  10.4 us
    all_gather x1, blocking collectives, local(): lax.all_gather(keys, 'ctx', axis=0, tiled=True)  9.66 us
    all_gather x1, blocking collectives, local(): lax.all_gather(values, 'ctx', axis=0, tiled=True)  9.66 us
    all_gather x1, blocking collectives, local(): lax.all_gather(jnp.transpose(lse_heads), 'ctx', axis=0, tiled=True)  8.94 us
    all_gather x1, blocking collectives, local(): lax.all_gather(delta_rows, 'ctx', axis=0, tiled=True)  8.18 us
  transfers between devices with their start and end apart: 4, of which 2 were waited for; matrix products, arithmetic and copies ran while one was open for 5% of the time, Pallas kernels for 0%

commit v1 on v0

--- a/solution.py
+++ b/solution.py
@@ -9,6 +9,24 @@
 SQRT_HALF = 0.7071067811865476
 INV_ROOT_TAU = 0.3989422804014327
 EPSILON = 1e-05
+
+
+def collect(shard, axis, dim):
+    ways, here, step = (lax.axis_size(axis), lax.axis_index(axis), shard.shape[dim])
+    shape = [n * ways if d == dim else n for d, n in enumerate(shard.shape)]
+    full = lax.dynamic_update_slice_in_dim(
+        jnp.zeros(shape, shard.dtype), shard, here * step, axis=dim
+    )
+    going_up = going_down = shard
+    for far in range(1, ways // 2 + 1):
+        going_up = lax.ppermute(going_up, axis, [(d, (d + 1) % ways) for d in range(ways)])
+        full = lax.dynamic_update_slice_in_dim(full, going_up, (here - far) % ways * step, axis=dim)
+        if 2 * far < ways:
+            going_down = lax.ppermute(going_down, axis, [(d, (d - 1) % ways) for d in range(ways)])
+            full = lax.dynamic_update_slice_in_dim(
+                full, going_down, (here + far) % ways * step, axis=dim
+            )
+    return full
 
 
 def from_behind(value, axis, steps):
@@ -137,7 +155,7 @@
     )
     query_grad = (query_accum * scale).astype(jnp.bfloat16).reshape(count, HEADS * HEAD_DIM)
     all_lse, all_delta = (
-        lax.all_gather(jnp.transpose(lse_heads), "ctx", axis=0, tiled=True),
+        collect(jnp.transpose(lse_heads), "ctx", 0),
         lax.all_gather(delta_rows, "ctx", axis=0, tiled=True),
     )
 

time: 180 us -> 187 us (1.039)
  local copies, waits for them, and re-layouts: 21.9 us -> 30.4 us
  starting transfers between devices: 3.59 us -> 11.7 us
  blocking collectives: 59.4 us -> 51.7 us
  matrix products: 22.3 us -> 19.2 us
    all_gather x1 -> x0, blocking collectives: 8.94 us -> none  [local(): lax.all_gather(jnp.transpose(lse_heads), 'ctx', axis=0, tiled=True)]
    ppermute x0 -> x7, starting transfers between devices: none -> 8.04 us  [the longest x3 7.28 us: collect(): lax.ppermute(going_down, axis, [(d, (d - 1) % ways) for d in range(ways)])]
    dynamic_update_slice x0 -> x8, local copies, waits for them, and re-layouts: none -> 6.64 us  [the longest x4 3.32 us: collect(): lax.dynamic_update_slice_in_dim(full, going_up, (here - far) % ways * ste...]
    all_gather x1, blocking collectives: 8.18 us -> 10.2 us  [local(): lax.all_gather(delta_rows, 'ctx', axis=0, tiled=True)]
    unnamed x56 -> x59, local copies, waits for them, and re-layouts: 6.82 us -> 8.17 us
  transfers between devices with their start and end apart: 4 -> 11, of which waited for: 2 -> 3; matrix products, arithmetic and copies ran while one was open for 5% -> 16% of each run, Pallas kernels for 0% -> 0%
where the time goes in v1:
time: 187 us; the launch traced here: 185 us
  waiting for transfers between devices  54.6 us (29%)
  blocking collectives  51.7 us (28%)
  local copies, waits for them, and re-layouts  30.4 us (16%)
  matrix products  19.2 us (10%)
  between operations  14.6 us (8%)
  starting transfers between devices  11.7 us (6%)
  other arithmetic  3.13 us (2%)
    reduce_scatter x1, waiting for transfers between devices, local(): lax.psum_scatter(kernel_terms.astype(jnp.bfloat16), 'ctx', scatter_dimens...  35.8 us
    unnamed x3, waiting for transfers between devices  18.7 us
    all_gather x1, blocking collectives, local(): lax.all_gather(upstream, 'ctx', axis=0, tiled=True)  12.5 us
    all_gather x1, blocking collectives, local(): lax.all_gather(values, 'ctx', axis=0, tiled=True)  10.3 us
    all_gather x1, blocking collectives, local(): lax.all_gather(delta_rows, 'ctx', axis=0, tiled=True)  10.2 us
    all_gather x1, blocking collectives, local(): lax.all_gather(keys, 'ctx', axis=0, tiled=True)  9.82 us
    all_gather x1, blocking collectives, local(): lax.all_gather(queries, 'ctx', axis=0, tiled=True)  8.84 us
    unnamed x59, local copies, waits for them, and re-layouts  8.17 us
  transfers between devices with their start and end apart: 11, of which 3 were waited for; matrix products, arithmetic and copies ran while one was open for 16% of the time, Pallas kernels for 0%

profile of v1, /device:TPU:0, one launch (start us, length us, event | category | flops | bytes accessed | tf_op | source)
XLA Modules:
  0.0 185.3 jit_solution(2318902725415570372)
XLA Ops:
  7.2 0.9 slice_bitcast_fusion
  8.1 1.3 collective-permute-start
  9.4 1.0 reshape_squeeze.6
  10.7 1.5 copy.41
  12.2 12.5 %all-gather = bf16[1,512,384]{2,1,0:T(8,128)(2,1)S(1)} all-gather(bf16[1,64,384]{2,1,0:T(8,128)(2,1)} %param.13), channel_id=2, replica_groups=mesh['dp'=4,'ctx'=8] {'ctx'}, dimensions={1}, use_global_device_ids=true | all-gather | bytes 442368 | tf_op jit(solution)/shard_map/all_gather | solution.py:201
  25.8 1.2 fusion.90
  28.7 0.6 copy-done.14
  29.3 9.8 %all_gather.17 = bf16[512,384]{1,0:T(8,128)(2,1)} all-gather(bf16[64,384]{1,0:T(8,128)(2,1)S(1)} %convolution_convert_fusion.8), channel_id=1, replica_groups=mesh['dp'=4,'ctx'=8] {'ctx'}, dimensions={0}, use_global_device_ids=true | all-gather | bytes 442368 | tf_op jit(solution)/shard_map/all_gather | solution.py:152
  39.1 1.9 %copy.38 = bf16[512,384]{0,1:T(8,128)(2,1)} copy(bf16[512,384]{1,0:T(8,128)(2,1)} %all_gather.17) | data formatting | bytes 786432 | tf_op jit(solution)/shard_map/all_gather | solution.py:152
  41.3 0.8 reshape.115
  42.0 1.4 fusion.93
  44.8 2.3 %collective-permute-start.2 = (f32[64,6]{0,1:T(8,128)S(1)}, f32[64,6]{0,1:T(8,128)}, u32[]{:S(2)}, u32[]{:S(2)}) collective-permute-start(f32[64,6]{0,1:T(8,128)S(1)} %get-tuple-element.62), channel_id=1, source_target_pairs={{0,7},{1,0},{2,1},{3,2},{4,3},{5,4},{6,5},{7,6},{8,15},{9,8},{10,9... | collective-permute-start | bytes 4616 | tf_op jit(solution)/shard_map/ppermute | solution.py:25
  47.9 10.3 %all_gather.18 = bf16[512,384]{1,0:T(8,128)(2,1)} all-gather(bf16[64,384]{1,0:T(8,128)(2,1)S(1)} %convolution_convert_fusion.6), channel_id=1, replica_groups=mesh['dp'=4,'ctx'=8] {'ctx'}, dimensions={0}, use_global_device_ids=true | all-gather | bytes 442368 | tf_op jit(solution)/shard_map/all_gather | solution.py:153
  58.2 1.9 %copy.40 = bf16[512,384]{0,1:T(8,128)(2,1)} copy(bf16[512,384]{1,0:T(8,128)(2,1)} %all_gather.18) | data formatting | bytes 786432 | tf_op jit(solution)/shard_map/all_gather | solution.py:153
  60.1 1.7 fusion.18
  61.8 2.3 %fusion.17 = bf16[6,64,64]{2,1,0:T(8,128)(2,1)} fusion(bf16[512,6,64]{0,2,1:T(8,128)(2,1)} %bitcast.151, bf16[512,6,64]{0,2,1:T(8,128)(2,1)} %bitcast.155, bf16[64,6,64]{0,2,1:T(8,128)(2,1)} %bitcast.162, f32[6,64,512]{2,1,0:T(8,128)S(1)} %get-tuple-element.67, f32[6,64]{1,0:T(8,128)S(1)} %bitcast.165, f32[6,64]{1,0:T(8,128)S(1)} %log_add_fusion), kind=kOutput, calls=%fused_computation.28 | convolution fusion | flops 51167232 | bytes 1674240 | tf_op jit(solution)/shard_map/while/body/eval_jaxpr/hqk,khe->qhe/dot_general | solution.py:140
  64.2 8.8 %all_gather.19 = bf16[512,384]{1,0:T(8,128)(2,1)S(1)} all-gather(bf16[64,384]{1,0:T(8,128)(2,1)} %copy-done.15), channel_id=1, replica_groups=mesh['dp'=4,'ctx'=8] {'ctx'}, dimensions={0}, use_global_device_ids=true | all-gather | bytes 442368 | tf_op jit(solution)/shard_map/all_gather | solution.py:200
  73.0 1.6 reshape.119
  74.6 0.9 copy.43
  75.9 1.3 convolution_multiply_fusion
  77.2 2.3 %collective-permute-start.4 = (f32[64,6]{0,1:T(8,128)}, f32[64,6]{0,1:T(8,128)}, u32[]{:S(2)}, u32[]{:S(2)}) collective-permute-start(f32[64,6]{0,1:T(8,128)} %collective-permute-done.2), channel_id=1, source_target_pairs={{0,7},{1,0},{2,1},{3,2},{4,3},{5,4},{6,5},{7,6},{8,15},{9,8},{10,9... | collective-permute-start | bytes 4616 | tf_op jit(solution)/shard_map/ppermute | solution.py:25
  79.7 2.1 %fusion.96 = f32[64,768]{1,0:T(8,128)} fusion(bf16[64,384]{0,1:T(8,128)(2,1)} %bitcast.160, bf16[768,384]{1,0:T(8,128)(2,1)} %param.10), kind=kOutput, calls=%fused_computation.137 | convolution fusion | flops 37748736 | bytes 835584 | tf_op jit(solution)/shard_map/tk,dk->td/dot_general | solution.py:206
  81.8 2.6 %collective-permute-start.6 = (f32[64,6]{0,1:T(8,128)}, f32[64,6]{0,1:T(8,128)}, u32[]{:S(2)}, u32[]{:S(2)}) collective-permute-start(f32[64,6]{0,1:T(8,128)} %collective-permute-done.4), channel_id=1, source_target_pairs={{0,7},{1,0},{2,1},{3,2},{4,3},{5,4},{6,5},{7,6},{8,15},{9,8},{10,9... | collective-permute-start | bytes 4616 | tf_op jit(solution)/shard_map/ppermute | solution.py:25
  84.4 10.2 %all-gather.1 = f32[8,64,6]{1,2,0:T(8,128)} all-gather(f32[1,64,6]{1,2,0:T(8,128)S(1)} %bitcast.166), channel_id=1, replica_groups=mesh['dp'=4,'ctx'=8] {'ctx'}, dimensions={0}, use_global_device_ids=true | all-gather | bytes 13824 | tf_op jit(solution)/shard_map/all_gather | solution.py:159
  94.7 1.6 reshape.120
  96.3 1.4 copy.47
  97.6 1.4 reshape.128
  99.0 0.8 dynamic_update_slice.24
  99.8 0.9 dynamic_update_slice.25
  100.7 0.9 dynamic_update_slice.26
  101.6 0.8 dynamic_update_slice.27
  102.3 0.8 dynamic_update_slice.28
  103.1 0.9 dynamic_update_slice.29
  104.0 0.9 dynamic_update_slice.30
  104.9 0.8 dynamic_update_slice.31
  106.0 0.7 copy.48
  106.7 1.7 reshape.123
  108.3 2.1 %fusion.16 = bf16[6,64,64]{2,1,0:T(8,128)(2,1)} fusion(bf16[512,6,64]{0,2,1:T(8,128)(2,1)} %bitcast.149, bf16[512,6,64]{0,2,1:T(8,128)(2,1)S(1)} %bitcast.147, f32[6,512,64]{1,2,0:T(8,128)S(1)} %convolution_multiply_fusion, f32[6,512]{1,0:T(8,128)} %bitcast.163, f32[6,512]{1,0:T(8,128)S(1)} %bitcast.159, bf16[64,6,64]{2,1,0:T(8,128)(2,1)} %reshape.120), kind=kOutput, calls=%fused_computation.27 | convolution fusion | flops 51167232 | bytes 1695744 | tf_op jit(solution)/shard_map/while/body/eval_jaxpr/hqk,qhe->khe/dot_general | solution.py:184
  110.5 1.5 convolution_add_fusion.1
  112.0 1.8 fusion.89
  115.0 1.3 pad_maximum_fusion
  116.4 2.3 %collective-permute-start.8 = (bf16[1,512]{1,0:T(2,128)(2,1)S(1)}, bf16[1,512]{1,0:T(2,128)(2,1)S(1)}, u32[]{:S(2)}, u32[]{:S(2)}) collective-permute-start(bf16[1,512]{1,0:T(2,128)(2,1)S(1)} %slice.53), channel_id=1, source_target_pairs={{0,1},{1,2},{2,3},{3,4},{4,5},{5,6},{6,7},{8,9},{9,10},{10,11},{11... | collective-permute-start | bytes 3080 | tf_op jit(solution)/shard_map/ppermute | solution.py:35
  119.2 35.8 %reduce-scatter.5.cloned.1.call-done = bf16[192,512]{1,0:T(8,128)(2,1)} async-done(((bf16[1536,512]{1,0:T(8,128)(2,1)}), bf16[192,512]{1,0:T(8,128)(2,1)}) %reduce-scatter.5.cloned.1.call-update) | async-done | bytes 196624 | tf_op jit(solution)/shard_map/reduce_scatter | solution.py:241
  155.0 1.8 copy.51
  157.5 0.7 convert_element_type.89
  158.2 18.7 %reduce-scatter.7.cloned.1.call-done = bf16[128,192]{1,0:T(8,128)(2,1)} async-done(((bf16[512,192]{1,0:T(8,128)(2,1)}), bf16[128,192]{1,0:T(8,128)(2,1)}) %reduce-scatter.7.cloned.1.call-update) | async-done | bytes 49168
  176.9 0.9 copy.52
  177.8 0.7 convert_element_type.88
  (100 shorter events, 8.4 us)
Async XLA Ops:
  7.2 20.9 %copy-start = (bf16[512,768]{1,0:T(8,128)(2,1)S(1)}, bf16[512,768]{1,0:T(8,128)(2,1)}, u32[]{:S(2)}) copy-start(bf16[512,768]{1,0:T(8,128)(2,1)} %param.9) | copy-start | bytes 2359300
  7.2 17.5 %copy-start.1 = (bf16[3,512,512]{2,1,0:T(8,128)(2,1)S(1)}, bf16[3,512,512]{2,1,0:T(8,128)(2,1)}, u32[]{:S(2)}) copy-start(bf16[3,512,512]{2,1,0:T(8,128)(2,1)} %param.8) | copy-start | bytes 4718596
  7.2 147.8 %reduce-scatter.5.cloned.1.call-start = ((), (), s32[]{:S(2)}) async-start(), calls=%async_computation.2 | async-start | bytes 1769472 | tf_op jit(solution)/shard_map/reduce_scatter | solution.py:241
  8.1 17.4 %collective-permute-start = (bf16[1,512]{1,0:T(2,128)(2,1)S(1)}, bf16[1,512]{1,0:T(2,128)(2,1)S(1)}, u32[]{:S(2)}, u32[]{:S(2)}) collective-permute-start(bf16[1,512]{1,0:T(2,128)(2,1)S(1)} %slice_bitcast_fusion), channel_id=1, source_target_pairs={{1,0},{2,1},{3,2},{4,3},{5,4},{6,5},{7,6},{9,8},{10,9},{11,10},{12... | collective-permute-start | bytes 3080 | tf_op jit(solution)/shard_map/ppermute | solution.py:35
  10.5 14.6 %copy-start.9 = (bf16[64,1,512]{2,1,0:T(2,128)(2,1)}, bf16[64,1,512]{2,1,0:T(2,128)(2,1)S(1)}, u32[]{:S(2)}) copy-start(bf16[64,1,512]{2,1,0:T(2,128)(2,1)S(1)} %get-tuple-element.61) | copy-start | bytes 196612
  10.5 14.6 %copy-start.11 = (bf16[64,1,512]{2,1,0:T(2,128)(2,1)}, bf16[64,1,512]{2,1,0:T(2,128)(2,1)S(1)}, u32[]{:S(2)}) copy-start(bf16[64,1,512]{2,1,0:T(2,128)(2,1)S(1)} %get-tuple-element.60) | copy-start | bytes 196612
  25.2 0.6 copy-start.16
  25.4 1.6 copy-start.25
  25.8 2.6 %copy-start.3 = (bf16[768,384]{1,0:T(8,128)(2,1)S(1)}, bf16[768,384]{1,0:T(8,128)(2,1)}, u32[]{:S(2)}) copy-start(bf16[768,384]{1,0:T(8,128)(2,1)} %param.11) | copy-start | bytes 1769476
  27.0 1.6 copy-start.5
  27.0 14.0 %copy-start.2 = (bf16[768,384]{1,0:T(8,128)(2,1)S(1)}, bf16[768,384]{1,0:T(8,128)(2,1)}, u32[]{:S(2)}) copy-start(bf16[768,384]{1,0:T(8,128)(2,1)} %param.10) | copy-start | bytes 1769476
  27.1 0.5 copy-start.20
  27.6 0.5 copy-start.22
  28.4 13.6 %copy-start.7 = (bf16[64,768]{1,0:T(8,128)(2,1)}, bf16[64,768]{1,0:T(8,128)(2,1)S(1)}, u32[]{:S(2)}) copy-start(bf16[64,768]{1,0:T(8,128)(2,1)S(1)} %convolution_convert_fusion.4) | copy-start | bytes 294916
  28.7 0.6 copy-start.14
  41.2 0.8 copy-start.15
  42.0 5.0 %copy-start.4 = (bf16[768,384]{1,0:T(8,128)(2,1)S(1)}, bf16[768,384]{1,0:T(8,128)(2,1)}, u32[]{:S(2)}) copy-start(bf16[768,384]{1,0:T(8,128)(2,1)} %param.12) | copy-start | bytes 1769476
  42.0 5.0 %copy-start.8 = (bf16[64,768]{1,0:T(8,128)(2,1)S(1)}, bf16[64,768]{1,0:T(8,128)(2,1)}, u32[]{:S(2)}) copy-start(bf16[64,768]{1,0:T(8,128)(2,1)} %copy-done.7) | copy-start | bytes 294916
  44.4 17.5 %copy-start.19 = (f32[64,6]{0,1:T(8,128)}, f32[64,6]{0,1:T(8,128)S(1)}, u32[]{:S(2)}) copy-start(f32[64,6]{0,1:T(8,128)S(1)} %get-tuple-element.62) | copy-start | bytes 4612
  44.4 31.1 %collective-permute-start.1 = (f32[64,6]{0,1:T(8,128)S(1)}, f32[64,6]{0,1:T(8,128)}, u32[]{:S(2)}, u32[]{:S(2)}) collective-permute-start(f32[64,6]{0,1:T(8,128)S(1)} %get-tuple-element.62), channel_id=1, source_target_pairs={{0,1},{1,2},{2,3},{3,4},{4,5},{5,6},{6,7},{7,0},{8,9},{9,10},{10,1... | collective-permute-start | bytes 4616 | tf_op jit(solution)/shard_map/ppermute | solution.py:22
  44.8 32.4 %collective-permute-start.2 = (f32[64,6]{0,1:T(8,128)S(1)}, f32[64,6]{0,1:T(8,128)}, u32[]{:S(2)}, u32[]{:S(2)}) collective-permute-start(f32[64,6]{0,1:T(8,128)S(1)} %get-tuple-element.62), channel_id=1, source_target_pairs={{0,7},{1,0},{2,1},{3,2},{4,3},{5,4},{6,5},{7,6},{8,15},{9,8},{10,9... | collective-permute-start | bytes 4616 | tf_op jit(solution)/shard_map/ppermute | solution.py:25
  47.3 0.6 copy-start.13
  75.5 4.1 %collective-permute-start.3 = (f32[64,6]{0,1:T(8,128)}, f32[64,6]{0,1:T(8,128)S(1)}, u32[]{:S(2)}, u32[]{:S(2)}) collective-permute-start(f32[64,6]{0,1:T(8,128)} %collective-permute-done.1), channel_id=1, source_target_pairs={{0,1},{1,2},{2,3},{3,4},{4,5},{5,6},{6,7},{7,0},{8,9},{9,10},{10,1... | collective-permute-start | bytes 4616 | tf_op jit(solution)/shard_map/ppermute | solution.py:22
  77.2 4.6 %collective-permute-start.4 = (f32[64,6]{0,1:T(8,128)}, f32[64,6]{0,1:T(8,128)}, u32[]{:S(2)}, u32[]{:S(2)}) collective-permute-start(f32[64,6]{0,1:T(8,128)} %collective-permute-done.2), channel_id=1, source_target_pairs={{0,7},{1,0},{2,1},{3,2},{4,3},{5,4},{6,5},{7,6},{8,15},{9,8},{10,9... | collective-permute-start | bytes 4616 | tf_op jit(solution)/shard_map/ppermute | solution.py:25
  79.7 18.0 %copy-start.24 = (f32[64,6]{0,1:T(8,128)}, f32[64,6]{0,1:T(8,128)S(1)}, u32[]{:S(2)}) copy-start(f32[64,6]{0,1:T(8,128)S(1)} %collective-permute-done.3) | copy-start | bytes 4612
  79.7 4.8 %collective-permute-start.5 = (f32[64,6]{0,1:T(8,128)S(1)}, f32[64,6]{0,1:T(8,128)}, u32[]{:S(2)}, u32[]{:S(2)}) collective-permute-start(f32[64,6]{0,1:T(8,128)S(1)} %collective-permute-done.3), channel_id=1, source_target_pairs={{0,1},{1,2},{2,3},{3,4},{4,5},{5,6},{6,7},{7,0},{8,9},{9,10},{10,1... | collective-permute-start | bytes 4616 | tf_op jit(solution)/shard_map/ppermute | solution.py:22
  81.8 22.2 %collective-permute-start.6 = (f32[64,6]{0,1:T(8,128)}, f32[64,6]{0,1:T(8,128)}, u32[]{:S(2)}, u32[]{:S(2)}) collective-permute-start(f32[64,6]{0,1:T(8,128)} %collective-permute-done.4), channel_id=1, source_target_pairs={{0,7},{1,0},{2,1},{3,2},{4,3},{5,4},{6,5},{7,6},{8,15},{9,8},{10,9... | collective-permute-start | bytes 4616 | tf_op jit(solution)/shard_map/ppermute | solution.py:25
  84.4 20.5 %collective-permute-start.7 = (f32[64,6]{0,1:T(8,128)}, f32[64,6]{0,1:T(8,128)}, u32[]{:S(2)}, u32[]{:S(2)}) collective-permute-start(f32[64,6]{0,1:T(8,128)} %collective-permute-done.5), channel_id=1, source_target_pairs={{0,1},{1,2},{2,3},{3,4},{4,5},{5,6},{6,7},{7,0},{8,9},{9,10},{10,1... | collective-permute-start | bytes 4616 | tf_op jit(solution)/shard_map/ppermute | solution.py:22
  110.5 3.3 %copy-start.6 = (f32[64,512]{1,0:T(8,128)S(1)}, f32[64,512]{1,0:T(8,128)}, u32[]{:S(2)}) copy-start(f32[64,512]{1,0:T(8,128)} %copy-done.5) | copy-start | bytes 393220
  110.5 3.3 %copy-start.18 = (f32[64,512]{1,0:T(8,128)S(1)}, f32[64,512]{1,0:T(8,128)}, u32[]{:S(2)}) copy-start(f32[64,512]{1,0:T(8,128)} %get-tuple-element.65) | copy-start | bytes 393220
  110.5 3.4 %copy-start.21 = (f32[64]{0:T(128)S(1)}, f32[64]{0:T(128)}, u32[]{:S(2)}) copy-start(f32[64]{0:T(128)} %copy-done.20) | copy-start | bytes 772
  110.5 3.4 %copy-start.23 = (f32[64]{0:T(128)S(1)}, f32[64]{0:T(128)}, u32[]{:S(2)}) copy-start(f32[64]{0:T(128)} %copy-done.22) | copy-start | bytes 772
  110.5 3.5 %copy-start.12 = (bf16[64,1,512]{2,1,0:T(2,128)(2,1)S(1)}, bf16[64,1,512]{2,1,0:T(2,128)(2,1)}, u32[]{:S(2)}) copy-start(bf16[64,1,512]{2,1,0:T(2,128)(2,1)} %copy-done.11) | copy-start | bytes 196612
  112.0 2.3 %copy-start.10 = (bf16[64,1,512]{2,1,0:T(2,128)(2,1)S(1)}, bf16[64,1,512]{2,1,0:T(2,128)(2,1)}, u32[]{:S(2)}) copy-start(bf16[64,1,512]{2,1,0:T(2,128)(2,1)} %copy-done.9) | copy-start | bytes 196612
  112.0 2.7 %copy-start.17 = (bf16[63,1,512]{2,0,1:T(8,128)(2,1)S(1)}, bf16[63,1,512]{2,0,1:T(8,128)(2,1)}, u32[]{:S(2)}) copy-start(bf16[63,1,512]{2,0,1:T(8,128)(2,1)} %copy-done.16) | copy-start | bytes 193540
  112.0 2.7 %copy-start.26 = (bf16[1,512]{1,0:T(2,128)(2,1)S(1)}, bf16[1,512]{1,0:T(2,128)(2,1)}, u32[]{:S(2)}) copy-start(bf16[1,512]{1,0:T(2,128)(2,1)} %copy-done.25) | copy-start | bytes 3076
  116.3 60.6 %reduce-scatter.7.cloned.1.call-start = ((), (), s32[]{:S(2)}) async-start(), calls=%async_computation.3 | async-start | bytes 327680
  116.4 40.4 %collective-permute-start.8 = (bf16[1,512]{1,0:T(2,128)(2,1)S(1)}, bf16[1,512]{1,0:T(2,128)(2,1)S(1)}, u32[]{:S(2)}, u32[]{:S(2)}) collective-permute-start(bf16[1,512]{1,0:T(2,128)(2,1)S(1)} %slice.53), channel_id=1, source_target_pairs={{0,1},{1,2},{2,3},{3,4},{4,5},{5,6},{6,7},{8,9},{9,10},{10,11},{11... | collective-permute-start | bytes 3080 | tf_op jit(solution)/shard_map/ppermute | solution.py:35
Sparse Core Ops, SparseCore 0:
  116.4 38.5 reduce-scatter.4
  157.2 19.6 reduce-scatter.6
